TPU v7x, 256 devices: a whole 4x4x8 slice. The times are simulated.
256 devices in a mesh: blk: 16 (over x_lo, y, core), rep: 16 (over x_hi, z).
Axes of the slice: x: 4 (x_hi: 2, x_lo: 2; x = x_hi * 2 + x_lo), y: 4, z: 8, core: 2. Of those that a mesh axis runs over, the one named last changes fastest.
Arguments:
- features: bfloat16 [65536, 256], P(('blk', 'rep')), may hold values from -6 to 6
- tiles: bfloat16 [256, 16, 16, 128, 128], P(('blk', 'rep'))
- tile_rows: int32 [256, 16, 16], P(('blk', 'rep')), may hold values from 0 to 31
- tile_cols: int32 [256, 16, 16], P(('blk', 'rep')), may hold values from 0 to 1
- tile_counts: int32 [256, 16], P(('blk', 'rep')), may hold values from 0 to 16, as said below
- self_weight: bfloat16 [256, 256], replicated, may hold values from -0.375 to 0.375
- neigh_weight: bfloat16 [256, 256], replicated, may hold values from -0.375 to 0.375
- bias: float32 [256], replicated, may hold values from -3 to 3
- out_grad: bfloat16 [65536, 256], P(('blk', 'rep')), may hold values from -6 to 6
Outputs:
- output: bfloat16 [65536, 256], P(('blk', 'rep'))
- grad_features: bfloat16 [65536, 256], P(('blk', 'rep'))
- grad_self: float32 [256, 256], replicated
- grad_neigh: float32 [256, 256], replicated
- grad_bias: float32 [256], replicated
Inputs may be any that keep to these rules, and one draw needn't show every extreme that they name: `tile_counts`: in every draw one device has all 16 slots live for every source block; other devices carry skewed loads.
All inputs are finite; a program needn't handle non-finite values.
Results may differ from a plain program's by a relative error of at most 0.0075.
Values may be sent and summed in bfloat16 or wider, within the bound.
A program may use at most 64 MiB of HBM per device.

v0:
```python
import jax
import jax.numpy as jnp
from jax import lax
from jax.sharding import PartitionSpec as P


def from_behind(value, axis, steps):
    count = lax.axis_size(axis)
    pairs = [(source, (source + steps) % count) for source in range(count)]
    return lax.ppermute(value, axis, pairs)


def forward_batched(tiles_at, rows_at, cols_at, count_at, current, tile_len, block_tiles):
    slot_count = tiles_at.shape[0]
    row_tiles = current.shape[0] // tile_len
    source = current.reshape(row_tiles, tile_len, current.shape[1])
    pick = (cols_at[:, None] == jnp.arange(row_tiles, dtype=jnp.int32)[None, :]).astype(
        jnp.bfloat16
    )
    picked = jnp.einsum("sk,ktd->std", pick, source, preferred_element_type=jnp.float32).astype(
        jnp.bfloat16
    )
    product = jnp.einsum("sij,sjd->sid", tiles_at, picked, preferred_element_type=jnp.float32)
    live = (jnp.arange(slot_count, dtype=jnp.int32) < count_at).astype(jnp.float32)
    place = (rows_at[:, None] == jnp.arange(block_tiles, dtype=jnp.int32)[None, :]).astype(
        jnp.float32
    )
    place = place * live[:, None]
    return jnp.einsum("sn,sid->nid", place, product, precision=lax.Precision.HIGHEST)


def backward_batched(tiles_at, rows_at, cols_at, count_at, spread, row_tiles):
    slot_count = tiles_at.shape[0]
    block_tiles = spread.shape[0]
    select = (rows_at[:, None] == jnp.arange(block_tiles, dtype=jnp.int32)[None, :]).astype(
        jnp.bfloat16
    )
    picked = jnp.einsum("sn,nid->sid", select, spread, preferred_element_type=jnp.float32).astype(
        jnp.bfloat16
    )
    product = jnp.einsum("sji,sjd->sid", tiles_at, picked, preferred_element_type=jnp.float32)
    live = (jnp.arange(slot_count, dtype=jnp.int32) < count_at).astype(jnp.float32)
    place = (cols_at[:, None] == jnp.arange(row_tiles, dtype=jnp.int32)[None, :]).astype(
        jnp.float32
    )
    place = place * live[:, None]
    return jnp.einsum("sk,sid->kid", place, product, precision=lax.Precision.HIGHEST)


def body(
    features, tiles, tile_rows, tile_cols, tile_counts, self_weight, neigh_weight, bias, out_grad
):
    cycle_len = lax.axis_size("blk")
    rep_len = lax.axis_size("rep")
    block_index = lax.axis_index("blk")
    rows_dev = features.shape[0]
    width = features.shape[1]
    tile_len = tiles.shape[-1]
    row_tiles = rows_dev // tile_len
    block_tiles = rep_len * row_tiles
    my_tiles = tiles[0]
    my_rows = tile_rows[0]
    my_cols = tile_cols[0]
    my_counts = tile_counts[0]

    def forward_term(column, current):
        tiles_at = lax.dynamic_index_in_dim(my_tiles, column, 0, False)
        rows_at = lax.dynamic_index_in_dim(my_rows, column, 0, False)
        cols_at = lax.dynamic_index_in_dim(my_cols, column, 0, False)
        count_at = lax.dynamic_index_in_dim(my_counts, column, 0, False)
        return forward_batched(tiles_at, rows_at, cols_at, count_at, current, tile_len, block_tiles)

    def forward_step(step, carry):
        current, total = carry
        column = (block_index - step) % cycle_len
        total = total + forward_term(column, current)
        current = from_behind(current, "blk", 1)
        return (current, total)

    start = jnp.zeros((block_tiles, tile_len, width), jnp.float32)
    current, total = lax.fori_loop(0, cycle_len - 1, forward_step, (features, start))
    total = total + forward_term((block_index - (cycle_len - 1)) % cycle_len, current)
    partial_value = total.reshape(block_tiles * tile_len, width)
    summed = lax.psum(partial_value, "rep")
    own_rows = lax.dynamic_slice_in_dim(summed, lax.axis_index("rep") * rows_dev, rows_dev, 0)
    agg_low = own_rows.astype(jnp.bfloat16)
    preact = (
        jnp.dot(features, self_weight, preferred_element_type=jnp.float32)
        + jnp.dot(agg_low, neigh_weight, preferred_element_type=jnp.float32)
        + bias
    )
    sigmoid_pre = jax.nn.sigmoid(preact)
    output = (preact * sigmoid_pre).astype(jnp.bfloat16)
    dpre = (
        out_grad.astype(jnp.float32) * sigmoid_pre * (1.0 + preact * (1.0 - sigmoid_pre))
    ).astype(jnp.bfloat16)
    local_self = jnp.einsum("nd,ne->de", features, dpre, preferred_element_type=jnp.float32)
    local_neigh = jnp.einsum("nd,ne->de", agg_low, dpre, preferred_element_type=jnp.float32)
    local_bias = jnp.sum(dpre.astype(jnp.float32), axis=0)
    grad_self, grad_neigh, grad_bias = lax.psum(
        (local_self, local_neigh, local_bias), ("blk", "rep")
    )
    dagg = jnp.einsum("ne,de->nd", dpre, neigh_weight, preferred_element_type=jnp.float32).astype(
        jnp.bfloat16
    )
    gathered = lax.all_gather(dagg, "rep", axis=0, tiled=True)
    spread = gathered.reshape(block_tiles, tile_len, width)

    def backward_term(column):
        tiles_at = lax.dynamic_index_in_dim(my_tiles, column, 0, False)
        rows_at = lax.dynamic_index_in_dim(my_rows, column, 0, False)
        cols_at = lax.dynamic_index_in_dim(my_cols, column, 0, False)
        count_at = lax.dynamic_index_in_dim(my_counts, column, 0, False)
        return backward_batched(tiles_at, rows_at, cols_at, count_at, spread, row_tiles)

    def backward_step(step, carried):
        column = (block_index - 1 - step) % cycle_len
        return from_behind(carried + backward_term(column), "blk", 1)

    carried = lax.fori_loop(
        0, cycle_len - 1, backward_step, jnp.zeros((row_tiles, tile_len, width), jnp.float32)
    )
    carried = carried + backward_term(block_index % cycle_len)
    grad_features = (
        jnp.einsum("ne,de->nd", dpre, self_weight, preferred_element_type=jnp.float32)
        + carried.reshape(rows_dev, width)
    ).astype(jnp.bfloat16)
    return (output, grad_features, grad_self, grad_neigh, grad_bias)


def solution(mesh):
    return jax.shard_map(
        body,
        mesh=mesh,
        in_specs=(
            P(("blk", "rep"), None),
            P(("blk", "rep"), None, None, None, None),
            P(("blk", "rep"), None, None),
            P(("blk", "rep"), None, None),
            P(("blk", "rep"), None),
            P(),
            P(),
            P(),
            P(("blk", "rep"), None),
        ),
        out_specs=(P(("blk", "rep"), None), P(("blk", "rep"), None), P(), P(), P()),
        check_vma=False,
    )
```

profile of v0, /device:TPU:2, one launch (start us, length us, event | category | flops | bytes accessed | tf_op | source)
XLA Modules:
  0.0 823.6 jit_solution(10696027552938043336)
XLA Ops:
  11.1 189.6 %while.34 = (s32[]{:T(128)}, bf16[256,256]{1,0:T(8,128)(2,1)S(1)}, f32[32,128,256]{2,0,1:T(8,128)}, s32[]{:T(128)}, s32[16,16]{1,0:T(8,128)}, /*index=5*/s32[16]...) while((s32[]{:T(128)}, bf16[256,256]{1,0:T(8,128)(2,1)S(1)}, ...), condition=%wide.region_1.2_spmd.clone, body=%wide.region_0.1_spmd.clone.sunk | while | flops 339739712 | bytes 16122714 | solution.py:81
  15.9 5.8 select_add_fusion.2
  28.1 7.3 select_add_fusion.2
  40.2 7.3 select_add_fusion.2
  53.9 7.3 select_add_fusion.2
  66.1 7.3 select_add_fusion.2
  79.5 7.3 select_add_fusion.2
  91.6 7.3 select_add_fusion.2
  105.7 7.3 select_add_fusion.2
  117.9 7.3 select_add_fusion.2
  130.0 7.3 select_add_fusion.2
  142.1 7.3 select_add_fusion.2
  155.7 7.3 select_add_fusion.2
  167.9 7.3 select_add_fusion.2
  181.3 7.3 select_add_fusion.2
  193.4 7.3 select_add_fusion.2
  203.5 5.9 convolution_add_fusion
  209.4 4.4 copy.16
  213.8 109.0 %all-reduce.5 = bf16[4096,256]{1,0:T(8,128)(2,1)S(1)} all-reduce(f32[4096,256]{1,0:T(8,128)} %bitcast.101), channel_id=1, replica_groups=mesh['blk'=16,'rep'=16] {'rep'}, use_global_device_ids=true, to_apply=%region_2.3 | all-reduce | flops 1048576 | bytes 6291456 | tf_op jit(solution)/shard_map/psum | solution.py:84
  326.8 75.9 %psum.31 = f32[256]{0:T(256)} all-reduce(f32[256]{0:T(256)S(1)} %get-tuple-element.481), channel_id=1, replica_groups=mesh['blk'=16,'rep'=16] {'blk','rep'}, use_global_device_ids=true, to_apply=%region_8.9 | all-reduce | flops 256 | bytes 2048 | tf_op jit(solution)/shard_map/psum | solution.py:100
  403.3 174.4 %all-reduce.4.cloned.1.call-done = (f32[256,256]{0,1:T(8,128)}, f32[256,256]{1,0:T(8,128)}) async-done(((f32[256,256]{0,1:T(8,128)}, f32[256,256]{1,0:T(8,128)}), (f32[256,256]{0,1:T(8,128)}, f32[256,256]{1,0:T(8,128)})) %all-reduce.4.cloned.1.call-update) | async-done | bytes 524304 | tf_op jit(solution)/shard_map/psum | solution.py:100
  579.5 2.8 fusion.43
  582.3 3.1 fusion.52
  585.5 225.3 %while.33 = (s32[]{:T(128)}, f32[2,128,256]{2,0,1:T(2,128)S(1)}, s32[]{:T(128)}, s32[16,16]{1,0:T(8,128)}, s32[16]{0:T(128)S(1)}, /*index=5*/bf16[16,16,128,128]...) while((s32[]{:T(128)}, f32[2,128,256]{2,0,1:T(2,128)S(1)}, ...), condition=%wide.region_4.5_spmd, body=%wide.region_3.4_spmd.sunk | while | flops 180421232 | bytes 10486608 | solution.py:120
  592.6 7.9 collective-permute-done
  605.3 2.2 fusion.123
  607.7 7.9 collective-permute-done
  620.3 2.2 fusion.123
  622.7 7.9 collective-permute-done
  635.3 2.2 fusion.123
  637.7 7.9 collective-permute-done
  650.4 2.2 fusion.123
  652.7 7.9 collective-permute-done
  665.4 2.2 fusion.123
  667.7 7.9 collective-permute-done
  680.4 2.2 fusion.123
  682.7 7.9 collective-permute-done
  695.4 2.2 fusion.123
  697.8 7.9 collective-permute-done
  710.4 2.2 fusion.123
  712.8 7.9 collective-permute-done
  727.8 7.9 collective-permute-done
  742.8 7.9 collective-permute-done
  757.8 7.9 collective-permute-done
  772.8 7.9 collective-permute-done
  787.8 7.9 collective-permute-done
  802.9 7.9 collective-permute-done
  810.7 3.8 fusion.46
  (256 shorter events, 183.2 us)
Async XLA Ops:
  8.0 315.0 %copy-start = (bf16[256,256]{1,0:T(8,128)(2,1)S(1)}, bf16[256,256]{1,0:T(8,128)(2,1)}, u32[]{:S(2)}) copy-start(bf16[256,256]{1,0:T(8,128)(2,1)} %param.19) | copy-start | bytes 393220
  8.0 569.7 %all-reduce.4.cloned.1.call-start = ((), (), s32[]{:S(2)}) async-start(), calls=%async_computation.1 | async-start | bytes 1048576 | tf_op jit(solution)/shard_map/psum | solution.py:100
  11.1 10.6 %collective-permute-start.1 = (bf16[256,256]{1,0:T(8,128)(2,1)S(1)}, bf16[256,256]{1,0:T(8,128)(2,1)S(1)}, u32[]{:S(2)}, u32[]{:S(2)}) collective-permute-start(bf16[256,256]{1,0:T(8,128)(2,1)S(1)} %copy.75), channel_id=1, source_target_pairs={{0,16},{16,32},{32,48},{48,64},{64,80},{80,96},{96,112},{112,128},... | collective-permute-start | bytes 393224 | tf_op jit(solution)/shard_map/while/body/eval_jaxpr/ppermute | solution.py:10
  21.7 13.7 %collective-permute-start.1 = (bf16[256,256]{1,0:T(8,128)(2,1)S(1)}, bf16[256,256]{1,0:T(8,128)(2,1)S(1)}, u32[]{:S(2)}, u32[]{:S(2)}) collective-permute-start(bf16[256,256]{1,0:T(8,128)(2,1)S(1)} %copy.75), channel_id=1, source_target_pairs={{0,16},{16,32},{32,48},{48,64},{64,80},{80,96},{96,112},{112,128},... | collective-permute-start | bytes 393224 | tf_op jit(solution)/shard_map/while/body/eval_jaxpr/ppermute | solution.py:10
  35.4 12.1 %collective-permute-start.1 = (bf16[256,256]{1,0:T(8,128)(2,1)S(1)}, bf16[256,256]{1,0:T(8,128)(2,1)S(1)}, u32[]{:S(2)}, u32[]{:S(2)}) collective-permute-start(bf16[256,256]{1,0:T(8,128)(2,1)S(1)} %copy.75), channel_id=1, source_target_pairs={{0,16},{16,32},{32,48},{48,64},{64,80},{80,96},{96,112},{112,128},... | collective-permute-start | bytes 393224 | tf_op jit(solution)/shard_map/while/body/eval_jaxpr/ppermute | solution.py:10
  47.6 13.7 %collective-permute-start.1 = (bf16[256,256]{1,0:T(8,128)(2,1)S(1)}, bf16[256,256]{1,0:T(8,128)(2,1)S(1)}, u32[]{:S(2)}, u32[]{:S(2)}) collective-permute-start(bf16[256,256]{1,0:T(8,128)(2,1)S(1)} %copy.75), channel_id=1, source_target_pairs={{0,16},{16,32},{32,48},{48,64},{64,80},{80,96},{96,112},{112,128},... | collective-permute-start | bytes 393224 | tf_op jit(solution)/shard_map/while/body/eval_jaxpr/ppermute | solution.py:10
  61.3 12.1 %collective-permute-start.1 = (bf16[256,256]{1,0:T(8,128)(2,1)S(1)}, bf16[256,256]{1,0:T(8,128)(2,1)S(1)}, u32[]{:S(2)}, u32[]{:S(2)}) collective-permute-start(bf16[256,256]{1,0:T(8,128)(2,1)S(1)} %copy.75), channel_id=1, source_target_pairs={{0,16},{16,32},{32,48},{48,64},{64,80},{80,96},{96,112},{112,128},... | collective-permute-start | bytes 393224 | tf_op jit(solution)/shard_map/while/body/eval_jaxpr/ppermute | solution.py:10
  73.4 13.4 %collective-permute-start.1 = (bf16[256,256]{1,0:T(8,128)(2,1)S(1)}, bf16[256,256]{1,0:T(8,128)(2,1)S(1)}, u32[]{:S(2)}, u32[]{:S(2)}) collective-permute-start(bf16[256,256]{1,0:T(8,128)(2,1)S(1)} %copy.75), channel_id=1, source_target_pairs={{0,16},{16,32},{32,48},{48,64},{64,80},{80,96},{96,112},{112,128},... | collective-permute-start | bytes 393224 | tf_op jit(solution)/shard_map/while/body/eval_jaxpr/ppermute | solution.py:10
  86.8 12.1 %collective-permute-start.1 = (bf16[256,256]{1,0:T(8,128)(2,1)S(1)}, bf16[256,256]{1,0:T(8,128)(2,1)S(1)}, u32[]{:S(2)}, u32[]{:S(2)}) collective-permute-start(bf16[256,256]{1,0:T(8,128)(2,1)S(1)} %copy.75), channel_id=1, source_target_pairs={{0,16},{16,32},{32,48},{48,64},{64,80},{80,96},{96,112},{112,128},... | collective-permute-start | bytes 393224 | tf_op jit(solution)/shard_map/while/body/eval_jaxpr/ppermute | solution.py:10
  99.0 14.1 %collective-permute-start.1 = (bf16[256,256]{1,0:T(8,128)(2,1)S(1)}, bf16[256,256]{1,0:T(8,128)(2,1)S(1)}, u32[]{:S(2)}, u32[]{:S(2)}) collective-permute-start(bf16[256,256]{1,0:T(8,128)(2,1)S(1)} %copy.75), channel_id=1, source_target_pairs={{0,16},{16,32},{32,48},{48,64},{64,80},{80,96},{96,112},{112,128},... | collective-permute-start | bytes 393224 | tf_op jit(solution)/shard_map/while/body/eval_jaxpr/ppermute | solution.py:10
  113.1 12.1 %collective-permute-start.1 = (bf16[256,256]{1,0:T(8,128)(2,1)S(1)}, bf16[256,256]{1,0:T(8,128)(2,1)S(1)}, u32[]{:S(2)}, u32[]{:S(2)}) collective-permute-start(bf16[256,256]{1,0:T(8,128)(2,1)S(1)} %copy.75), channel_id=1, source_target_pairs={{0,16},{16,32},{32,48},{48,64},{64,80},{80,96},{96,112},{112,128},... | collective-permute-start | bytes 393224 | tf_op jit(solution)/shard_map/while/body/eval_jaxpr/ppermute | solution.py:10
  125.2 12.1 %collective-permute-start.1 = (bf16[256,256]{1,0:T(8,128)(2,1)S(1)}, bf16[256,256]{1,0:T(8,128)(2,1)S(1)}, u32[]{:S(2)}, u32[]{:S(2)}) collective-permute-start(bf16[256,256]{1,0:T(8,128)(2,1)S(1)} %copy.75), channel_id=1, source_target_pairs={{0,16},{16,32},{32,48},{48,64},{64,80},{80,96},{96,112},{112,128},... | collective-permute-start | bytes 393224 | tf_op jit(solution)/shard_map/while/body/eval_jaxpr/ppermute | solution.py:10
  137.3 12.1 %collective-permute-start.1 = (bf16[256,256]{1,0:T(8,128)(2,1)S(1)}, bf16[256,256]{1,0:T(8,128)(2,1)S(1)}, u32[]{:S(2)}, u32[]{:S(2)}) collective-permute-start(bf16[256,256]{1,0:T(8,128)(2,1)S(1)} %copy.75), channel_id=1, source_target_pairs={{0,16},{16,32},{32,48},{48,64},{64,80},{80,96},{96,112},{112,128},... | collective-permute-start | bytes 393224 | tf_op jit(solution)/shard_map/while/body/eval_jaxpr/ppermute | solution.py:10
  149.5 13.6 %collective-permute-start.1 = (bf16[256,256]{1,0:T(8,128)(2,1)S(1)}, bf16[256,256]{1,0:T(8,128)(2,1)S(1)}, u32[]{:S(2)}, u32[]{:S(2)}) collective-permute-start(bf16[256,256]{1,0:T(8,128)(2,1)S(1)} %copy.75), channel_id=1, source_target_pairs={{0,16},{16,32},{32,48},{48,64},{64,80},{80,96},{96,112},{112,128},... | collective-permute-start | bytes 393224 | tf_op jit(solution)/shard_map/while/body/eval_jaxpr/ppermute | solution.py:10
  163.1 12.1 %collective-permute-start.1 = (bf16[256,256]{1,0:T(8,128)(2,1)S(1)}, bf16[256,256]{1,0:T(8,128)(2,1)S(1)}, u32[]{:S(2)}, u32[]{:S(2)}) collective-permute-start(bf16[256,256]{1,0:T(8,128)(2,1)S(1)} %copy.75), channel_id=1, source_target_pairs={{0,16},{16,32},{32,48},{48,64},{64,80},{80,96},{96,112},{112,128},... | collective-permute-start | bytes 393224 | tf_op jit(solution)/shard_map/while/body/eval_jaxpr/ppermute | solution.py:10
  175.2 13.4 %collective-permute-start.1 = (bf16[256,256]{1,0:T(8,128)(2,1)S(1)}, bf16[256,256]{1,0:T(8,128)(2,1)S(1)}, u32[]{:S(2)}, u32[]{:S(2)}) collective-permute-start(bf16[256,256]{1,0:T(8,128)(2,1)S(1)} %copy.75), channel_id=1, source_target_pairs={{0,16},{16,32},{32,48},{48,64},{64,80},{80,96},{96,112},{112,128},... | collective-permute-start | bytes 393224 | tf_op jit(solution)/shard_map/while/body/eval_jaxpr/ppermute | solution.py:10
  188.6 12.1 %collective-permute-start.1 = (bf16[256,256]{1,0:T(8,128)(2,1)S(1)}, bf16[256,256]{1,0:T(8,128)(2,1)S(1)}, u32[]{:S(2)}, u32[]{:S(2)}) collective-permute-start(bf16[256,256]{1,0:T(8,128)(2,1)S(1)} %copy.75), channel_id=1, source_target_pairs={{0,16},{16,32},{32,48},{48,64},{64,80},{80,96},{96,112},{112,128},... | collective-permute-start | bytes 393224 | tf_op jit(solution)/shard_map/while/body/eval_jaxpr/ppermute | solution.py:10
  213.8 109.0 %copy-start.2 = (bf16[256,256]{1,0:T(8,128)(2,1)S(1)}, bf16[256,256]{1,0:T(8,128)(2,1)}, u32[]{:S(2)}) copy-start(bf16[256,256]{1,0:T(8,128)(2,1)} %param.13) | copy-start | bytes 393220
  213.8 109.0 %copy-start.3 = (bf16[256,256]{1,0:T(8,128)(2,1)S(1)}, bf16[256,256]{1,0:T(8,128)(2,1)}, u32[]{:S(2)}) copy-start(bf16[256,256]{1,0:T(8,128)(2,1)} %param.18) | copy-start | bytes 393220
  213.8 109.2 %copy-start.6 = (bf16[256,256]{1,0:T(8,128)(2,1)S(1)}, bf16[256,256]{1,0:T(8,128)(2,1)}, u32[]{:S(2)}) copy-start(bf16[256,256]{1,0:T(8,128)(2,1)} %param.21) | copy-start | bytes 393220
  213.8 109.2 %copy-start.7 = (f32[256]{0:T(256)S(1)}, f32[256]{0:T(256)}, u32[]{:S(2)}) copy-start(f32[256]{0:T(256)} %param.20) | copy-start | bytes 3076
  325.9 253.6 %all-gather.2.cloned.1.call-start = ((), (), s32[]{:S(2)}) async-start(), calls=%async_computation | async-start | bytes 2228224 | tf_op jit(solution)/shard_map/all_gather | solution.py:106
  582.3 3.1 copy-start.1
  582.3 3.1 copy-start.5
  592.6 8.0 collective-permute-start
  607.6 8.0 collective-permute-start
  622.6 8.0 collective-permute-start
  637.6 8.0 collective-permute-start
  652.6 8.0 collective-permute-start
  667.6 8.0 collective-permute-start
  682.6 8.0 collective-permute-start
  697.7 8.0 collective-permute-start
  712.7 8.0 collective-permute-start
  727.7 8.0 collective-permute-start
  742.7 8.0 collective-permute-start
  757.7 8.0 collective-permute-start
  772.7 8.0 collective-permute-start
  787.7 8.0 collective-permute-start
  802.8 8.0 collective-permute-start
  810.7 4.7 copy-start.4
Sparse Core Ops, SparseCore 0:
  326.0 251.6 all-reduce.3
Sparse Core Ops, SparseCore 1:
  329.5 82.1 all-gather.1
where the time goes:
time: 827 us; the launch traced here: 824 us
  waiting for transfers between devices  293 us (35%)
  matrix products  237 us (29%)
  blocking collectives  185 us (22%)
  local copies, waits for them, and re-layouts  58.9 us (7%)
  other arithmetic  20.6 us (2%)
  between operations  15.7 us (2%)
  starting transfers between devices  12.4 us (1%)
    psum x1, waiting for transfers between devices, body(): lax.psum((local_self, local_neigh, local_bias), ('blk', 'rep'))  174 us
    ppermute x30, waiting for transfers between devices, from_behind(): return lax.ppermute(value, axis, pairs)  118 us
    dot_general x16, matrix products, forward_batched(): jnp.einsum('sn,sid->nid', place, product, precision=lax.Precision.HIGHEST)  114 us
    psum x1, blocking collectives, body(): summed = lax.psum(partial_value, 'rep')  109 us
    psum x1, blocking collectives, body(): lax.psum((local_self, local_neigh, local_bias), ('blk', 'rep'))  75.9 us
    dot_general x16, matrix products, backward_batched(): jnp.einsum('sk,sid->kid', place, product, precision=lax.Precision.HIGHEST)  37.5 us
    dot_general x16, matrix products, backward_batched(): jnp.einsum('sji,sjd->sid', tiles_at, picked, preferred_element_type=jnp.f...  26.5 us
    dot_general x16, matrix products, forward_batched(): jnp.einsum('sij,sjd->sid', tiles_at, picked, preferred_element_type=jnp.f...  25.2 us
  transfers between devices with their start and end apart: 32, of which 16 were waited for; matrix products, arithmetic and copies ran while one was open for 22% of the time, Pallas kernels for 0%

commit v1 on v0

v1 whole, which is shorter than its diff:
```python
import types

import jax
import jax.numpy as jnp
from jax import lax
from jax.experimental import pallas as pl
from jax.experimental.pallas import tpu as pltpu
from jax.sharding import PartitionSpec as P

BF, F32, I32 = jnp.bfloat16, jnp.float32, jnp.int32
MESH = pl.DeviceIdType.MESH
N_SRC = 16
SLOTS = 16
LIVE = N_SRC * SLOTS
TILE = 128
D = 256
SEGMENTS = 32
PAIRS = (LIVE + SEGMENTS) // 2
DEAD = 40
FWD_STEP = 24


def iota(shape, dim):
    return lax.broadcasted_iota(I32, shape, dim)


def ones_where(cond):
    return jnp.where(cond, 1.0, 0.0).astype(BF)


def dot(a, b, contract=((1,), (0,))):
    return lax.dot_general(a, b, (contract, ((), ())), preferred_element_type=F32)


def spread(table):
    slot = iota((LIVE, SLOTS), 0)
    picked = dot(ones_where(slot // SLOTS == iota((LIVE, SLOTS), 1)), table.astype(F32).astype(BF))
    own = jnp.where(slot % SLOTS == iota((LIVE, SLOTS), 1), picked, 0.0).astype(BF)
    ones = jnp.ones((LIVE, SLOTS), BF)
    return dot(own, ones, ((1,), (1,))), dot(ones, own, ((1,), (1,)))


def pair_table(key, other, by_source):
    down, along = spread(key)
    _, other_along = spread(other)
    before = (down == along) & (iota((LIVE, LIVE), 1) < iota((LIVE, LIVE), 0))
    place_in = dot(ones_where(before), jnp.ones((LIVE, 128), BF))
    member = down[:, :128] == iota((LIVE, 128), 1).astype(F32)
    size = dot(jnp.ones((LIVE, LIVE), BF), ones_where(member))
    pairs = jnp.floor((size + 1.0) * 0.5)
    group, later = iota((128, 128), 0), iota((128, 128), 1)
    if by_source:
        first_pair = dot(pairs.astype(BF), ones_where((later % 2 == 1) & (group == later - 1)))
        first_pair = first_pair + (9 * (iota((LIVE, 128), 1) // 2)).astype(F32)
    else:
        first_pair = dot(pairs.astype(BF), ones_where(group < later))
    own_first = dot(jnp.where(member & (iota((LIVE, 128), 1) < SEGMENTS), first_pair, 0.0).astype(BF), jnp.ones((128, 128), BF))
    place = 2.0 * own_first + place_in
    place = jnp.where(down[:, :128] < float(SEGMENTS), place, -1.0)
    place3 = jnp.concatenate([place, place, place], axis=1)
    place_in3 = jnp.concatenate([place_in, place_in, place_in], axis=1)
    held = place3 == iota((LIVE, 384), 1).astype(F32)
    held_low = ones_where(held)
    slot = iota((8, LIVE), 1)
    which = dot((slot - LIVE).astype(F32).astype(BF), held_low) + float(LIVE)
    what = dot(other_along[0:8].astype(BF), held_low)
    opens = dot(jnp.ones((8, LIVE), BF), ones_where(held & (place_in3 == 0.0)))
    row = iota((8, 384), 0)
    table = jnp.where(row == 0, which, jnp.where(row == 1, what, opens)).astype(I32)
    last = jnp.where(size > 0.0, first_pair + pairs, 0.0)[0:8].astype(I32)
    return table, last


def make_tables(rows, cols, counts, forward, forward_last, backward, backward_last):
    diagonal = iota((N_SRC, SLOTS), 0) == iota((N_SRC, SLOTS), 1)
    counted = jnp.where(diagonal, counts.astype(F32), 0.0).astype(BF)
    live = iota((N_SRC, SLOTS), 1).astype(F32) < dot(counted, jnp.ones((N_SRC, SLOTS), BF))
    source = 2 * iota((N_SRC, SLOTS), 0) + cols
    table, last = pair_table(jnp.where(live, rows, DEAD), source, False)
    forward[...] = table
    forward_last[...] = last
    table, last = pair_table(jnp.where(live, source, DEAD), rows, True)
    backward[...] = table
    backward_last[...] = last


def within(index, top):
    return jnp.minimum(jnp.maximum(index, 0), top)


def add_pairs(table, tiles, values, runs, first, count, running, transposed):
    for step in range(count):
        p = first + step
        left, right = within(table[0, 2 * p], LIVE), within(table[0, 2 * p + 1], LIVE)
        pick, pick_right = within(table[1, 2 * p], SEGMENTS - 1), within(table[1, 2 * p + 1], SEGMENTS - 1)
        held = jnp.concatenate([values[pick], values[pick_right]], axis=0)
        if transposed:
            product = dot(jnp.concatenate([tiles[left], tiles[right]], axis=0), held, ((0,), (0,)))
        else:
            product = dot(jnp.concatenate([tiles[left], tiles[right]], axis=1), held)
        running = product + jnp.where(table[2, 2 * p] > 0, 0.0, running)
        runs[p + 1] = running


class Wires:
    def __init__(self, send_sem, recv_sem, anyone):
        self.send_sem, self.recv_sem, self.anyone = send_sem, recv_sem, anyone
        self.names, self.pending = {}, []

    def copy(self, name, source, target, device):
        k = self.names.setdefault(name, len(self.names))
        return pltpu.make_async_remote_copy(
            src_ref=source, dst_ref=target, send_sem=self.send_sem.at[k], recv_sem=self.recv_sem.at[k],
            device_id=device, device_id_type=MESH)

    def push(self, name, source, target, device):
        copy = self.copy(name, source, target, device)
        copy.start()
        self.pending.append(copy)

    def take(self, name, target):
        self.copy(name, target, target, self.anyone).wait_recv()

    def flush(self):
        for copy in self.pending:
            copy.wait_send()
        self.pending = []


SCRATCH = dict(
    tiles=((LIVE + 1, TILE, TILE), BF), feats=((32, TILE, D), BF), runs=((PAIRS + 1, TILE, D), F32),
    daggs=((32, TILE, D), BF),
    fwd_v=((8, 384), I32), fwd_last_v=((8, 128), I32), bwd_v=((8, 384), I32), bwd_last_v=((8, 128), I32),
    self_part=((2, TILE, D), F32), aggs=((2, TILE, D), BF), dpres=((2, TILE, D), BF), base=((2, TILE, D), F32),
    a_up_out=((4, 2, TILE, D), BF), a_up_in=((4, 2, TILE, D), BF), a_down_out=((4, 2, TILE, D), BF), a_down_in=((4, 2, TILE, D), BF),
    b_up_out=((4, TILE, D), BF), b_up_in=((4, TILE, D), BF), b_down_out=((4, TILE, D), BF), b_down_in=((4, TILE, D), BF),
    bx_out=((8, TILE, D), BF), bx_in=((8, TILE, D), BF), ax_out=((TILE, D), BF), ax_in=((TILE, D), BF), a_own=((TILE, D), F32),
    core_out=((4, 2, 2, TILE, D), BF), core_in=((4, 2, 2, TILE, D), BF),
    y0_out=((2, 2, TILE, D), BF), y0_in=((2, 2, TILE, D), BF), y1_out=((2, 2, 2, TILE, D), BF), y1_in=((2, 2, 2, TILE, D), BF),
    rows=((1, N_SRC, SLOTS), I32), cols=((1, N_SRC, SLOTS), I32), counts=((1, N_SRC), I32), self_w=((D, D), BF), neigh_w=((D, D), BF),
    bias=((D,), F32), out_grad=((2 * TILE, D), BF), output=((2 * TILE, D), BF), grad_features=((2 * TILE, D), BF), grad_bias=((D,), F32),
    x_out=((2, TILE, D), BF), x_in=((2, TILE, D), BF),
    grads=((2, D, D), F32), grads_in=((D, D), F32), chip=((D, D), F32), quarter=((64, D), F32), y_parts=((3, 64, D), F32),
    x_parts=((3, 16, D), F32), z_parts=((8, 16, D), F32), full=((2, D, D), F32),
    bias_core=((2, 8, D), F32), bias_y=((4, 8, D), F32), bias_x=((4, 8, D), F32), bias_z=((8, 8, D), F32),
)
WIRES = 160


def layer_kernel(features, tiles_hbm, *rest):
    in_hbm, out_hbm, scratch = rest[:7], rest[7:12], rest[12:]
    s = types.SimpleNamespace(**dict(zip(SCRATCH, scratch)))
    fwd, fwd_last, bwd, bwd_last, send_sem, recv_sem, tile_sem, table_sem, in_sem, out_sem = scratch[len(SCRATCH):]
    tiles, feats, runs, daggs = s.tiles, s.feats, s.runs, s.daggs
    b, r = lax.axis_index("blk"), lax.axis_index("rep")
    xl, y, core = b // 8, lax.rem(b // 2, 4), lax.rem(b, 2)
    xh, z = r // 8, lax.rem(r, 8)
    x = 2 * xh + xl

    def block(xl, y, core):
        return xl * 8 + y * 2 + core

    def y_at(o):
        return lax.rem(y + o, 4)

    def z_at(o):
        return lax.rem(z + o, 8)

    def x_at(o):
        return lax.rem(x + o, 4)

    x_side, y_up, y_down, mate = (block(1 - xl, y, core), r), (block(xl, y_at(1), core), r), (block(xl, y_at(3), core), r), (block(xl, y, 1 - core), r)
    z_up, z_down, x_far = (b, xh * 8 + z_at(1)), (b, xh * 8 + z_at(7)), (b, (1 - xh) * 8 + z)
    y_peer = {o: (block(xl, y_at(o), core), r) for o in (1, 2, 3)}
    x_peer = {o: (block(lax.rem(x_at(o), 2), y, core), (x_at(o) // 2) * 8 + z) for o in (1, 2, 3)}
    z_peer = {o: (b, xh * 8 + z_at(o)) for o in range(1, 8)}
    w = Wires(send_sem, recv_sem, mate)

    load = pltpu.make_async_copy(tiles_hbm.at[0], tiles.at[pl.ds(0, LIVE)], tile_sem)
    held = (s.rows, s.cols, s.counts, s.self_w, s.neigh_w, s.bias, s.out_grad)
    reads = [pltpu.make_async_copy(features.at[pl.ds(half * TILE, TILE)], feats.at[2 * b + half], in_sem.at[half]) for half in range(2)]
    reads += [pltpu.make_async_copy(source, target, in_sem.at[2 + k]) for k, (source, target) in enumerate(zip(in_hbm, held))]
    barrier = pltpu.get_barrier_semaphore()
    partners = [mate, *y_peer.values(), *x_peer.values(), *z_peer.values()]
    for partner in partners:
        pl.semaphore_signal(barrier, inc=1, device_id=partner, device_id_type=MESH)
    for read in reads:
        read.start()
    load.start()
    rows, cols, counts, self_w, neigh_w, bias, out_grad = held
    output, grad_features, full = s.output, s.grad_features, s.full
    made = (output, grad_features, full.at[0], full.at[1], s.grad_bias)
    writes = [pltpu.make_async_copy(source, target, out_sem.at[k]) for k, (source, target) in enumerate(zip(made, out_hbm))]
    tiles[LIVE] = jnp.zeros((TILE, TILE), BF)
    runs[0] = jnp.zeros((TILE, D), F32)
    pl.semaphore_wait(barrier, len(partners))

    def feat(xl, y, core, half):
        return feats.at[2 * block(xl, y, core) + half]

    mates = []

    def spread_feat(name, where, device):
        w.push(name, feat(*where), feat(*where), device)

    def to_mate(xl, y, half):
        spread_feat("m%d" % len(mates), (xl, y, core, half), mate)
        mates.append((xl, y, half))

    def arrived(name, xl, y, half):
        w.take(name, feat(xl, y, core, half))
        to_mate(xl, y, half)

    other, before, behind, across = 1 - xl, y_at(3), y_at(1), y_at(2)
    for half in range(2):
        here = features.at[pl.ds(half * TILE, TILE)]
        there = feat(xl, y, core, half)
        w.push("fx%d" % half, here, there, x_side)
        w.push("fu0%d" % half, here, there, y_up)
        w.push("fd0%d" % half, here, there, y_down)
        w.push("m%d" % half, here, there, mate)
        mates.append((xl, y, half))

    for read in reads:
        read.wait()
    arrived("fx0", other, y, 0)
    spread_feat("fu10", (other, y, core, 0), y_up)
    spread_feat("fd10", (other, y, core, 0), y_down)
    arrived("fu00", xl, before, 0)
    spread_feat("fu2", (xl, before, core, 0), y_up)
    arrived("fx1", other, y, 1)
    spread_feat("fu11", (other, y, core, 1), y_up)
    spread_feat("fd11", (other, y, core, 1), y_down)
    arrived("fd01", xl, behind, 1)
    spread_feat("fd2", (xl, behind, core, 1), y_down)
    arrived("fd00", xl, behind, 0)
    arrived("fu01", xl, before, 1)
    arrived("fu10", other, before, 0)
    spread_feat("fu3", (other, before, core, 0), y_up)
    arrived("fd10", other, behind, 0)
    arrived("fd11", other, behind, 1)
    spread_feat("fd3", (other, behind, core, 1), y_down)
    arrived("fu11", other, before, 1)
    arrived("fu2", xl, across, 0)
    arrived("fd2", xl, across, 1)
    make_tables(rows[0], cols[0], counts[...], s.fwd_v, s.fwd_last_v, s.bwd_v, s.bwd_last_v)
    tables = [(s.fwd_v, fwd), (s.fwd_last_v, fwd_last), (s.bwd_v, bwd), (s.bwd_last_v, bwd_last)]
    tables = [pltpu.make_async_copy(here, there, table_sem.at[k]) for k, (here, there) in enumerate(tables)]
    for copy in tables:
        copy.start()
    for half in range(2):
        s.self_part[half] = dot(feats[2 * b + half], self_w[...]) + bias[...].reshape(1, D)
    arrived("fu3", other, across, 0)
    arrived("fd3", other, across, 1)
    for k, (side, at, half) in enumerate(mates):
        w.take("m%d" % k, feat(side, at, 1 - core, half))

    for copy in tables:
        copy.wait()
    load.wait()

    @pl.loop(0, PAIRS // FWD_STEP)
    def _(k):
        add_pairs(fwd, tiles, feats, runs, FWD_STEP * k, FWD_STEP, runs[FWD_STEP * k], False)

    def part(xh, z, half):
        return runs[within(fwd_last[0, (xh * 8 + z) * 2 + half], PAIRS)]

    a_up_out, a_up_in, a_down_out, a_down_in = s.a_up_out, s.a_up_in, s.a_down_out, s.a_down_in
    b_up_out, b_up_in, b_down_out, b_down_in = s.b_up_out, s.b_up_in, s.b_down_out, s.b_down_in
    bx_out, bx_in = s.bx_out, s.bx_in
    a_up_out[0, 0] = part(0, z_at(4), 0).astype(BF)
    w.push("au00", a_up_out.at[0, 0], a_up_in.at[0, 0], z_up)
    a_down_out[0, 1] = part(1, z_at(4), 0).astype(BF)
    w.push("ad01", a_down_out.at[0, 1], a_down_in.at[0, 1], z_down)
    offsets = (4, 3, 5, 2, 6, 1, 7, 0)

    def bx_send(j):
        bx_out[j] = part(1 - xh, z_at(offsets[j]), 1).astype(BF)
        w.push("bx%d" % j, bx_out.at[j], bx_in.at[j], x_far)

    bx_send(0)
    bx_send(1)
    a_up_out[1, 1] = part(1, z_at(3), 0).astype(BF)
    w.push("au11", a_up_out.at[1, 1], a_up_in.at[1, 1], z_up)
    a_down_out[1, 0] = part(0, z_at(5), 0).astype(BF)
    w.push("ad10", a_down_out.at[1, 0], a_down_in.at[1, 0], z_down)
    for j in range(2, 8):
        bx_send(j)
    low, high = pl.ds(0, TILE // 2), pl.ds(TILE // 2, TILE // 2)

    def a_step(k):
        for turn in ((0,) if k == 1 else (1, 0)):
            for name, out, into, device, o, half in (("au", a_up_out, a_up_in, z_up, 4 - k, 0), ("ad", a_down_out, a_down_in, z_down, 4 + k, 1)):
                side = half if turn == 0 else 1 - half
                w.take("%s%d%d" % (name, k - 1, side), into.at[k - 1, side])
                out[k, side] = (part(side, z_at(o), 0) + into[k - 1, side].astype(F32)).astype(BF)
                w.push("%s%d%d" % (name, k, side), out.at[k, side], into.at[k, side], device)

    def b_step(k):
        if k == 0:
            w.take("bx0", bx_in.at[0])
            value = (part(xh, z_at(4), 1) + bx_in[0].astype(F32)).astype(BF)
            b_up_out[0] = value
            b_down_out[0] = value
            w.push("bu0", b_up_out.at[0, low], b_up_in.at[0, low], z_up)
            w.push("bd0", b_down_out.at[0, high], b_down_in.at[0, high], z_down)
            return
        for name, out, into, device, j, rows_in in (("bu", b_up_out, b_up_in, z_up, 2 * k - 1, low), ("bd", b_down_out, b_down_in, z_down, 2 * k, high)):
            w.take("bx%d" % j, bx_in.at[j])
            w.take("%s%d" % (name, k - 1), into.at[0, rows_in] if k == 1 else into.at[k - 1])
            value = part(xh, z_at(offsets[j]), 1) + bx_in[j].astype(F32)
            if k > 1:
                value = value + into[k - 1].astype(F32)
            elif name == "bu":
                value = jnp.concatenate([value[:TILE // 2] + into[0, :TILE // 2].astype(F32), value[TILE // 2:]], axis=0)
            else:
                value = jnp.concatenate([value[:TILE // 2], value[TILE // 2:] + into[0, TILE // 2:].astype(F32)], axis=0)
            out[k] = value.astype(BF)
            w.push("%s%d" % (name, k), out.at[k], into.at[k], device)

    for k in (1, 2, 3):
        a_step(k)
        b_step(k - 1)
    for side in range(2):
        w.take("au3%d" % side, a_up_in.at[3, side])
        w.take("ad3%d" % side, a_down_in.at[3, side])

    def a_sum(side):
        return part(side, z, 0) + a_up_in[3, side].astype(F32) + a_down_in[3, side].astype(F32)

    s.ax_out[...] = a_sum(1 - xh).astype(BF)
    w.push("ax", s.ax_out, s.ax_in, x_far)
    b_step(3)
    s.a_own[...] = a_sum(xh)

    def layer(half, aggregate):
        here = slice(half * TILE, half * TILE + TILE)
        low_agg = aggregate.astype(BF)
        s.aggs[half] = low_agg
        preact = s.self_part[half] + dot(low_agg, neigh_w[...])
        gate = jax.nn.sigmoid(preact)
        output[here] = (preact * gate).astype(BF)
        dpre = (out_grad[here].astype(F32) * gate * (1.0 + preact * (1.0 - gate))).astype(BF)
        s.dpres[half] = dpre
        daggs[2 * r + half] = dot(dpre, neigh_w[...], ((1,), (1,))).astype(BF)

    def dagg(xh, z, half, rows=None):
        at = (xh * 8 + z) * 2 + half
        return daggs.at[at] if rows is None else daggs.at[at, rows]

    def spread_dagg(name, where, device, rows=None):
        w.push(name, dagg(*where, rows), dagg(*where, rows), device)

    w.take("ax", s.ax_in)
    layer(0, s.a_own[...] + s.ax_in[...].astype(F32))
    spread_dagg("gu1", (xh, z, 0), z_up)
    spread_dagg("gd1", (xh, z, 0), z_down)
    spread_dagg("x0", (xh, z, 0), x_far)
    w.take("bx7", bx_in.at[7])
    w.take("bu3", b_up_in.at[3])
    w.take("bd3", b_down_in.at[3])
    layer(1, part(xh, z, 1) + bx_in[7].astype(F32) + b_up_in[3].astype(F32) + b_down_in[3].astype(F32))
    spread_dagg("gx", (xh, z, 1), x_far)
    spread_dagg("hu1", (xh, z, 1), z_up)
    spread_dagg("hd1", (xh, z, 1), z_down)

    writes[0].start()
    aggs, dpres, grads = s.aggs, s.dpres, s.grads
    w.take("gx", dagg(1 - xh, z, 1))
    spread_dagg("iu1", (1 - xh, z, 1), z_up)
    spread_dagg("id1", (1 - xh, z, 1), z_down)

    def gather_step(k):
        for name, side, half in (("g", xh, 0), ("h", xh, 1), ("i", 1 - xh, 1)):
            for way, device, o, rows in (("u", z_up, 8 - k, low), ("d", z_down, k, high)):
                rows_in = rows if k == 4 else None
                w.take("%s%s%d" % (name, way, k), dagg(side, z_at(o), half, rows_in))
                if k < 4:
                    spread_dagg("%s%s%d" % (name, way, k + 1), (side, z_at(o), half), device, rows if k == 3 else None)
                if half == 0:
                    spread_dagg("x%s%d" % (way, k), (side, z_at(o), half), x_far, rows_in)

    quarter, chip, z_parts = s.quarter, s.chip, s.z_parts

    def weights_y():
        w.take("wc", s.grads_in)
        w.take("vc", bias_core.at[1])
        chip[...] = grads[core] + s.grads_in[...]
        bias_y[y] = bias_core[0] + bias_core[1]
        for o in (1, 2, 3):
            w.push("wy%d" % o, chip.at[pl.ds(64 * y_at(o), 64)], s.y_parts.at[o - 1], y_peer[o])
            w.push("vy%d" % o, bias_y.at[y], bias_y.at[y], y_peer[o])

    def weights_x():
        for o in (1, 2, 3):
            w.take("wy%d" % o, s.y_parts.at[o - 1])
            w.take("vy%d" % o, bias_y.at[y_at(4 - o)])
        quarter[...] = chip[pl.ds(64 * y, 64)] + s.y_parts[0] + s.y_parts[1] + s.y_parts[2]
        bias_x[x] = (bias_y[0] + bias_y[1]) + (bias_y[2] + bias_y[3])
        for o in (1, 2, 3):
            w.push("wx%d" % o, quarter.at[pl.ds(16 * x_at(o), 16)], s.x_parts.at[o - 1], x_peer[o])
            w.push("vx%d" % o, bias_x.at[x], bias_x.at[x], x_peer[o])

    def weights_z():
        for o in (1, 2, 3):
            w.take("wx%d" % o, s.x_parts.at[o - 1])
            w.take("vx%d" % o, bias_x.at[x_at(4 - o)])
        z_parts[z] = quarter[pl.ds(16 * x, 16)] + s.x_parts[0] + s.x_parts[1] + s.x_parts[2]
        bias_z[z] = (bias_x[0] + bias_x[1]) + (bias_x[2] + bias_x[3])
        for o in range(1, 8):
            w.push("wz%d" % o, z_parts.at[z], z_parts.at[z], z_peer[o])
            w.push("vz%d" % o, bias_z.at[z], bias_z.at[z], z_peer[o])

    def rows_of(y, x=None):
        return full.at[core, pl.ds(64 * y, 64)] if x is None else full.at[core, pl.ds(64 * y + 16 * x, 16)]

    def weights_total():
        for o in range(1, 8):
            w.take("wz%d" % o, z_parts.at[z_at(8 - o)])
            w.take("vz%d" % o, bias_z.at[z_at(8 - o)])
        total, bias_total = z_parts[0], bias_z[0]
        for o in range(1, 8):
            total, bias_total = total + z_parts[o], bias_total + bias_z[o]
        full[core, pl.ds(64 * y + 16 * x, 16)] = total
        s.grad_bias[...] = bias_total[0]
        writes[4].start()
        for o in (1, 2, 3):
            w.push("tx%d" % o, rows_of(y, x), rows_of(y, x), x_peer[o])

    def weights_back_y():
        for o in (1, 2, 3):
            w.take("tx%d" % o, rows_of(y, x_at(4 - o)))
        for o in (1, 2, 3):
            w.push("ty%d" % o, rows_of(y), rows_of(y), y_peer[o])

    def weights_back_core():
        for o in (1, 2, 3):
            w.take("ty%d" % o, rows_of(y_at(4 - o)))
        w.push("tc", full.at[core], full.at[core], mate)

    gather_step(1)
    dpre = dpres[...].reshape(2 * TILE, D)
    grads[0] = dot(feats[pl.ds(2 * b, 2)].reshape(2 * TILE, D), dpre, ((0,), (0,)))
    grads[1] = dot(aggs[...].reshape(2 * TILE, D), dpre, ((0,), (0,)))
    w.push("wc", grads.at[1 - core], s.grads_in, mate)
    bias_core, bias_y, bias_x, bias_z = s.bias_core, s.bias_y, s.bias_x, s.bias_z
    bias_core[0] = jnp.broadcast_to(jnp.sum(dpre.astype(F32), axis=0, keepdims=True), (8, D))
    w.push("vc", bias_core.at[0], bias_core.at[1], mate)
    for half in range(2):
        s.base[half] = dot(dpres[half], self_w[...], ((1,), (1,)))
    gather_step(2)
    weights_y()
    gather_step(3)
    weights_x()
    gather_step(4)
    weights_z()
    w.take("x0", dagg(1 - xh, z, 0))
    for k in (1, 2, 3, 4):
        w.take("xu%d" % k, dagg(1 - xh, z_at(8 - k), 0, low if k == 4 else None))
        w.take("xd%d" % k, dagg(1 - xh, z_at(k), 0, high if k == 4 else None))

    core_out, core_in = s.core_out, s.core_in
    y0_out, y0_in, y1_out, y1_in = s.y0_out, s.y0_in, s.y1_out, s.y1_in
    groups = (((1, 2), (0, 2)), ((1, 1), (1, 3)), ((0, 1), (0, 3)), ((1, 0), (0, 0)))

    def column(k):
        return (xl, other)[k]

    def back(k, o, to_core):
        to = block(column(k), y_at(o), to_core)
        add_pairs(bwd, tiles, daggs, runs, 9 * to, 9, jnp.zeros((TILE, D), F32), True)

    def term(k, o, to_core, half):
        return runs[within(bwd_last[0, 2 * block(column(k), y_at(o), to_core) + half], PAIRS)]

    def for_mate(g):
        for j, (k, o) in enumerate(groups[g]):
            back(k, o, 1 - core)
        for j, (k, o) in enumerate(groups[g]):
            for half in range(2):
                core_out[g, j, half] = term(k, o, 1 - core, half).astype(BF)
            w.push("k%d%d" % (g, j), core_out.at[g, j], core_in.at[g, j], mate)

    def for_own(g):
        for k, o in groups[g]:
            back(k, o, core)

    def chip_term(g, j, half):
        k, o = groups[g][j]
        return term(k, o, core, half) + core_in[g, j, half].astype(F32)

    def opposite():
        for j in range(2):
            k = groups[0][j][0]
            w.take("k0%d" % j, core_in.at[0, j])
            for way, device in enumerate((y_up, y_down)):
                y0_out[way, k] = chip_term(0, j, way).astype(BF)
                w.push("p%d%d" % (way, k), y0_out.at[way, k], y0_in.at[way, k], device)

    def neighbours(g):
        k = groups[g][0][0]
        for way, device in enumerate((y_up, y_down)):
            w.take("k%d%d" % (g, way), core_in.at[g, way])
            y1_out[way, k, 1 - way] = chip_term(g, way, 1 - way).astype(BF)
            w.push("q%d%d%d" % (way, k, 1 - way), y1_out.at[way, k, 1 - way], y1_in.at[way, k, 1 - way], device)
        for way, device in enumerate((y_up, y_down)):
            w.take("p%d%d" % (way, k), y0_in.at[way, k])
            y1_out[way, k, way] = (chip_term(g, way, way) + y0_in[way, k].astype(F32)).astype(BF)
            w.push("q%d%d%d" % (way, k, way), y1_out.at[way, k, way], y1_in.at[way, k, way], device)

    def column_sum(j, half):
        k = groups[3][j][0]
        for way in range(2):
            w.take("q%d%d%d" % (way, k, half), y1_in.at[way, k, half])
        return chip_term(3, j, half) + y1_in[0, k, half].astype(F32) + y1_in[1, k, half].astype(F32)

    for_mate(0)
    for_mate(1)
    for_own(0)
    opposite()
    weights_total()
    for_mate(2)
    for_own(1)
    neighbours(1)
    weights_back_y()
    for_mate(3)
    for_own(2)
    neighbours(2)
    weights_back_core()
    for_own(3)
    w.take("k30", core_in.at[3, 0])
    w.take("k31", core_in.at[3, 1])
    w.take("tc", full.at[1 - core])
    writes[2].start()
    writes[3].start()
    for half in range(2):
        s.x_out[half] = column_sum(0, half).astype(BF)
        w.push("x%d" % (half + 8), s.x_out.at[half], s.x_in.at[half], x_side)
    for half in range(2):
        s.base[half] = s.base[half] + column_sum(1, half)
    for half in range(2):
        w.take("x%d" % (half + 8), s.x_in.at[half])
        grad_features[half * TILE:half * TILE + TILE] = (s.base[half] + s.x_in[half].astype(F32)).astype(BF)
    writes[1].start()
    for write in writes:
        write.wait()
    w.flush()
    assert len(w.names) <= WIRES


OUTPUTS = [jax.ShapeDtypeStruct((2 * TILE, D), BF)] * 2 + [jax.ShapeDtypeStruct((D, D), F32)] * 2 + [jax.ShapeDtypeStruct((D,), F32)]


def hand_over(*refs):
    for k in range(5):
        refs[5 + k][...] = refs[k][...]


def body(features, tiles, tile_rows, tile_cols, tile_counts, self_weight, neigh_weight, bias, out_grad):
    anywhere = pl.BlockSpec(memory_space=pl.ANY)
    made = pl.pallas_call(
        layer_kernel,
        out_shape=OUTPUTS,
        in_specs=[anywhere] * 9,
        out_specs=[anywhere] * 5,
        scratch_shapes=[pltpu.VMEM(*spec) for spec in SCRATCH.values()] + [
            pltpu.SMEM((8, 384), I32), pltpu.SMEM((8, 128), I32), pltpu.SMEM((8, 384), I32), pltpu.SMEM((8, 128), I32),
            pltpu.SemaphoreType.DMA((WIRES,)), pltpu.SemaphoreType.DMA((WIRES,)),
            pltpu.SemaphoreType.DMA, pltpu.SemaphoreType.DMA((4,)), pltpu.SemaphoreType.DMA((9,)), pltpu.SemaphoreType.DMA((5,)),
        ],
        compiler_params=pltpu.CompilerParams(collective_id=0, has_side_effects=True, vmem_limit_bytes=56 << 20),
        name="sage_layer",
    )(features, tiles.reshape(1, LIVE, TILE, TILE), tile_rows, tile_cols, tile_counts, self_weight, neigh_weight, bias, out_grad)
    return pl.pallas_call(
        hand_over,
        out_shape=OUTPUTS,
        in_specs=[pl.BlockSpec(memory_space=pltpu.VMEM)] * 5,
        out_specs=[pl.BlockSpec(memory_space=pltpu.VMEM)] * 5,
        name="hand_over",
    )(*made)


def solution(mesh):
    split = ("blk", "rep")
    return jax.shard_map(
        body,
        mesh=mesh,
        in_specs=(P(split, None), P(split, None, None, None, None), P(split, None, None), P(split, None, None), P(split, None),
                  P(), P(), P(), P(split, None)),
        out_specs=(P(split, None), P(split, None), P(), P(), P()),
        check_vma=False,
    )
```

time: 827 us -> 98.4 us (0.12)
  waiting for transfers between devices: 293 us -> 0 us
  matrix products: 237 us -> 0 us
  blocking collectives: 185 us -> 0 us
  Pallas kernels: 0 us -> 97.1 us
  local copies, waits for them, and re-layouts: 58.9 us -> 0 us
  other arithmetic: 20.6 us -> 0 us
  between operations: 15.7 us -> 0.64 us
  starting transfers between devices: 12.4 us -> 0 us
    dot_general x102 -> x0, matrix products: 237 us -> none  [the longest x16 114 us: forward_batched(): jnp.einsum('sn,sid->nid', place, product, precision=lax.Precision.HIGHEST)]
    psum x2 -> x0, blocking collectives: 185 us -> none  [the longest x1 109 us: body(): summed = lax.psum(partial_value, 'rep')]
    psum x1 -> x0, waiting for transfers between devices: 174 us -> none  [body(): lax.psum((local_self, local_neigh, local_bias), ('blk', 'rep'))]
    ppermute x30 -> x0, waiting for transfers between devices: 118 us -> none  [from_behind(): return lax.ppermute(value, axis, pairs)]
    pallas_call x0 -> x2, Pallas kernels: none -> 97.1 us  [the longest x1 95.1 us: body(): pl.pallas_call(layer_kernel, out_shape=OUTPUTS, in_specs=[anywhere] * 9,...]
    dynamic_slice x31 -> x0, local copies, waits for them, and re-layouts: 28.6 us -> none  [the longest x15 18.6 us: forward_term(): count_at = lax.dynamic_index_in_dim(my_counts, column, 0, False)]
    eq x31 -> x0, local copies, waits for them, and re-layouts: 22.2 us -> none  [the longest x16 11.5 us: backward_batched(): cols_at[:, None] == jnp.arange(row_tiles, dtype=jnp.int32)[None, :]]
    convert_element_type x32 -> x0, other arithmetic: 20.6 us -> none  [the longest x16 10.4 us: forward_batched(): (jnp.arange(slot_count, dtype=jnp.int32) < count_at).astype(jnp.float32)]
  transfers between devices with their start and end apart: 32 -> 0, of which waited for: 16 -> 0; matrix products, arithmetic and copies ran while one was open for 22% -> 0% of each run, Pallas kernels for 0% -> 0%
where the time goes in v1:
time: 98.4 us; the launch traced here: 97.8 us
  Pallas kernels  97.1 us (99%)
    pallas_call x1, Pallas kernels, body(): pl.pallas_call(layer_kernel, out_shape=OUTPUTS, in_specs=[anywhere] * 9,...  95.1 us
    pallas_call x1, Pallas kernels, body(): pl.pallas_call(hand_over, out_shape=OUTPUTS, in_specs=[pl.BlockSpec(memor...  2.05 us

profile of v1, /device:TPU:2, one launch (start us, length us, event | category | flops | bytes accessed | tf_op | source)
XLA Modules:
  0.0 97.8 jit_solution(13812261699406508504)
XLA Ops:
  0.6 95.1 %sage_layer.1 = (bf16[256,256]{1,0:T(8,128)(2,1)}, bf16[256,256]{1,0:T(8,128)(2,1)}, f32[256,256]{1,0:T(8,128)}, f32[256,256]{1,0:T(8,128)}, f32[256]{0:T(256)}) custom-call(bf16[256,256]{1,0:T(8,128)(2,1)} %features.1, bf16[1,256,128,128]{3,2,1,0:T(8,128)(2,1)} %bitcast.1, s32[1,16,16]{2,1,0:T(8,128)} %rest_0_.1, s32[1,16,16]{2,1,0:T(8,128)} %rest_1_.1, ...), custom_call_target="tpu_custom_call" | custom-call | tf_op jit(solution)/shard_map/sage_layer/pallas_call | solution.py:562
  95.7 2.1 %hand_over.1 = (bf16[256,256]{1,0:T(8,128)(2,1)}, bf16[256,256]{1,0:T(8,128)(2,1)}, f32[256,256]{1,0:T(8,128)}, f32[256,256]{1,0:T(8,128)}, f32[256]{0:T(256)}) custom-call(bf16[256,256]{1,0:T(8,128)(2,1)} %get-tuple-element.10.refs_0_, bf16[256,256]{1,0:T(8,128)(2,1)} %get-tuple-element.11.refs_1_, f32[256,256]{1,0:T(8,128)} %get-tuple-element.12.refs_2_, ...), custom_call_target="tpu_custom_call" | custom-call | tf_op jit(solution)/shard_map/hand_over/pallas_call | solution.py:575

commit v2 on v1

--- a/solution.py
+++ b/solution.py
@@ -17,7 +17,7 @@
 SEGMENTS = 32
 PAIRS = (LIVE + SEGMENTS) // 2
 DEAD = 40
-FWD_STEP = 24
+FWD_STEP = 48
 
 
 def iota(shape, dim):
@@ -140,9 +140,8 @@
     rows=((1, N_SRC, SLOTS), I32), cols=((1, N_SRC, SLOTS), I32), counts=((1, N_SRC), I32), self_w=((D, D), BF), neigh_w=((D, D), BF),
     bias=((D,), F32), out_grad=((2 * TILE, D), BF), output=((2 * TILE, D), BF), grad_features=((2 * TILE, D), BF), grad_bias=((D,), F32),
     x_out=((2, TILE, D), BF), x_in=((2, TILE, D), BF),
-    grads=((2, D, D), F32), grads_in=((D, D), F32), chip=((D, D), F32), quarter=((64, D), F32), y_parts=((3, 64, D), F32),
-    x_parts=((3, 16, D), F32), z_parts=((8, 16, D), F32), full=((2, D, D), F32),
-    bias_core=((2, 8, D), F32), bias_y=((4, 8, D), F32), bias_x=((4, 8, D), F32), bias_z=((8, 8, D), F32),
+    grads=((2, 4, 64, D), F32), grads_in=((4, 64, D), F32), chip=((4, 72, D), F32), y_parts=((4, 72, D), F32), quarter=((4, 24, D), F32), x_parts=((4, 24, D), F32),
+    z_parts=((8, 24, D), F32), full=((2, D, D), F32), bias_core=((2, 8, D), F32),
 )
 WIRES = 160
 
@@ -171,8 +170,13 @@
 
     x_side, y_up, y_down, mate = (block(1 - xl, y, core), r), (block(xl, y_at(1), core), r), (block(xl, y_at(3), core), r), (block(xl, y, 1 - core), r)
     z_up, z_down, x_far = (b, xh * 8 + z_at(1)), (b, xh * 8 + z_at(7)), (b, (1 - xh) * 8 + z)
-    y_peer = {o: (block(xl, y_at(o), core), r) for o in (1, 2, 3)}
-    x_peer = {o: (block(lax.rem(x_at(o), 2), y, core), (x_at(o) // 2) * 8 + z) for o in (1, 2, 3)}
+    turns = [(i, j) for i in range(4) for j in range(4) if i or j]
+    plane = {(i, j): (block(lax.rem(x_at(i), 2), y_at(j), core), (x_at(i) // 2) * 8 + z) for i, j in turns}
+
+    def plane_part(i, j):
+        return 4 * y_at(j) + x_at(i)
+
+    own_part = 4 * y + x
     z_peer = {o: (b, xh * 8 + z_at(o)) for o in range(1, 8)}
     w = Wires(send_sem, recv_sem, mate)
 
@@ -181,7 +185,7 @@
     reads = [pltpu.make_async_copy(features.at[pl.ds(half * TILE, TILE)], feats.at[2 * b + half], in_sem.at[half]) for half in range(2)]
     reads += [pltpu.make_async_copy(source, target, in_sem.at[2 + k]) for k, (source, target) in enumerate(zip(in_hbm, held))]
     barrier = pltpu.get_barrier_semaphore()
-    partners = [mate, *y_peer.values(), *x_peer.values(), *z_peer.values()]
+    partners = [mate, *plane.values(), *z_peer.values()]
     for partner in partners:
         pl.semaphore_signal(barrier, inc=1, device_id=partner, device_id_type=MESH)
     for read in reads:
@@ -381,70 +385,61 @@
                 if half == 0:
                     spread_dagg("x%s%d" % (way, k), (side, z_at(o), half), x_far, rows_in)
 
-    quarter, chip, z_parts = s.quarter, s.chip, s.z_parts
+    chip, y_parts, quarter, x_parts, z_parts = s.chip, s.y_parts, s.quarter, s.x_parts, s.z_parts
 
     def weights_y():
         w.take("wc", s.grads_in)
         w.take("vc", bias_core.at[1])
-        chip[...] = grads[core] + s.grads_in[...]
-        bias_y[y] = bias_core[0] + bias_core[1]
+        chip[:, 0:64] = grads[core] + s.grads_in[...]
+        chip[:, 64:72] = jnp.broadcast_to((bias_core[0] + bias_core[1])[None], (4, 8, D))
+        y_parts[y] = chip[y]
         for o in (1, 2, 3):
-            w.push("wy%d" % o, chip.at[pl.ds(64 * y_at(o), 64)], s.y_parts.at[o - 1], y_peer[o])
-            w.push("vy%d" % o, bias_y.at[y], bias_y.at[y], y_peer[o])
+            w.push("wy%d" % o, chip.at[y_at(o)], y_parts.at[y], plane[0, o])
 
     def weights_x():
         for o in (1, 2, 3):
-            w.take("wy%d" % o, s.y_parts.at[o - 1])
-            w.take("vy%d" % o, bias_y.at[y_at(4 - o)])
-        quarter[...] = chip[pl.ds(64 * y, 64)] + s.y_parts[0] + s.y_parts[1] + s.y_parts[2]
-        bias_x[x] = (bias_y[0] + bias_y[1]) + (bias_y[2] + bias_y[3])
+            w.take("wy%d" % o, y_parts.at[y_at(4 - o)])
+        total = (y_parts[0] + y_parts[1]) + (y_parts[2] + y_parts[3])
+        quarter[:, 0:16] = total[0:64].reshape(4, 16, D)
+        quarter[:, 16:24] = jnp.broadcast_to(total[64:72][None], (4, 8, D))
+        x_parts[x] = quarter[x]
         for o in (1, 2, 3):
-            w.push("wx%d" % o, quarter.at[pl.ds(16 * x_at(o), 16)], s.x_parts.at[o - 1], x_peer[o])
-            w.push("vx%d" % o, bias_x.at[x], bias_x.at[x], x_peer[o])
+            w.push("wx%d" % o, quarter.at[x_at(o)], x_parts.at[x], plane[o, 0])
 
     def weights_z():
         for o in (1, 2, 3):
-            w.take("wx%d" % o, s.x_parts.at[o - 1])
-            w.take("vx%d" % o, bias_x.at[x_at(4 - o)])
-        z_parts[z] = quarter[pl.ds(16 * x, 16)] + s.x_parts[0] + s.x_parts[1] + s.x_parts[2]
-        bias_z[z] = (bias_x[0] + bias_x[1]) + (bias_x[2] + bias_x[3])
+            w.take("wx%d" % o, x_parts.at[x_at(4 - o)])
+        total = (x_parts[0] + x_parts[1]) + (x_parts[2] + x_parts[3])
+        z_parts[z] = total
         for o in range(1, 8):
             w.push("wz%d" % o, z_parts.at[z], z_parts.at[z], z_peer[o])
-            w.push("vz%d" % o, bias_z.at[z], bias_z.at[z], z_peer[o])
-
-    def rows_of(y, x=None):
-        return full.at[core, pl.ds(64 * y, 64)] if x is None else full.at[core, pl.ds(64 * y + 16 * x, 16)]
+
+    def rows_of(part):
+        return full.at[core, pl.ds(16 * part, 16)]
 
     def weights_total():
         for o in range(1, 8):
             w.take("wz%d" % o, z_parts.at[z_at(8 - o)])
-            w.take("vz%d" % o, bias_z.at[z_at(8 - o)])
-        total, bias_total = z_parts[0], bias_z[0]
+        total = z_parts[0]
         for o in range(1, 8):
-            total, bias_total = total + z_parts[o], bias_total + bias_z[o]
-        full[core, pl.ds(64 * y + 16 * x, 16)] = total
-        s.grad_bias[...] = bias_total[0]
+            total = total + z_parts[o]
+        full[core, pl.ds(16 * own_part, 16)] = total[0:16]
+        s.grad_bias[...] = total[16]
         writes[4].start()
-        for o in (1, 2, 3):
-            w.push("tx%d" % o, rows_of(y, x), rows_of(y, x), x_peer[o])
-
-    def weights_back_y():
-        for o in (1, 2, 3):
-            w.take("tx%d" % o, rows_of(y, x_at(4 - o)))
-        for o in (1, 2, 3):
-            w.push("ty%d" % o, rows_of(y), rows_of(y), y_peer[o])
+        for i, j in turns:
+            w.push("t%d%d" % (i, j), rows_of(own_part), rows_of(own_part), plane[i, j])
 
     def weights_back_core():
-        for o in (1, 2, 3):
-            w.take("ty%d" % o, rows_of(y_at(4 - o)))
+        for i, j in turns:
+            w.take("t%d%d" % (i, j), rows_of(plane_part(4 - i, 4 - j)))
         w.push("tc", full.at[core], full.at[core], mate)
 
     gather_step(1)
     dpre = dpres[...].reshape(2 * TILE, D)
-    grads[0] = dot(feats[pl.ds(2 * b, 2)].reshape(2 * TILE, D), dpre, ((0,), (0,)))
-    grads[1] = dot(aggs[...].reshape(2 * TILE, D), dpre, ((0,), (0,)))
+    grads[0] = dot(feats[pl.ds(2 * b, 2)].reshape(2 * TILE, D), dpre, ((0,), (0,))).reshape(4, 64, D)
+    grads[1] = dot(aggs[...].reshape(2 * TILE, D), dpre, ((0,), (0,))).reshape(4, 64, D)
     w.push("wc", grads.at[1 - core], s.grads_in, mate)
-    bias_core, bias_y, bias_x, bias_z = s.bias_core, s.bias_y, s.bias_x, s.bias_z
+    bias_core = s.bias_core
     bias_core[0] = jnp.broadcast_to(jnp.sum(dpre.astype(F32), axis=0, keepdims=True), (8, D))
     w.push("vc", bias_core.at[0], bias_core.at[1], mate)
     for half in range(2):
@@ -452,9 +447,8 @@
     gather_step(2)
     weights_y()
     gather_step(3)
+    gather_step(4)
     weights_x()
-    gather_step(4)
-    weights_z()
     w.take("x0", dagg(1 - xh, z, 0))
     for k in (1, 2, 3, 4):
         w.take("xu%d" % k, dagg(1 - xh, z_at(8 - k), 0, low if k == 4 else None))
@@ -517,32 +511,32 @@
 
     for_mate(0)
     for_mate(1)
+    weights_z()
     for_own(0)
     opposite()
-    weights_total()
     for_mate(2)
     for_own(1)
     neighbours(1)
-    weights_back_y()
+    weights_total()
     for_mate(3)
     for_own(2)
     neighbours(2)
-    weights_back_core()
     for_own(3)
     w.take("k30", core_in.at[3, 0])
     w.take("k31", core_in.at[3, 1])
-    w.take("tc", full.at[1 - core])
-    writes[2].start()
-    writes[3].start()
     for half in range(2):
         s.x_out[half] = column_sum(0, half).astype(BF)
         w.push("x%d" % (half + 8), s.x_out.at[half], s.x_in.at[half], x_side)
+    weights_back_core()
     for half in range(2):
         s.base[half] = s.base[half] + column_sum(1, half)
     for half in range(2):
         w.take("x%d" % (half + 8), s.x_in.at[half])
         grad_features[half * TILE:half * TILE + TILE] = (s.base[half] + s.x_in[half].astype(F32)).astype(BF)
     writes[1].start()
+    w.take("tc", full.at[1 - core])
+    writes[2].start()
+    writes[3].start()
     for write in writes:
         write.wait()
     w.flush()

time: 98.4 us -> 93.8 us (0.953)
  Pallas kernels: 97.1 us -> 93.1 us
    pallas_call x1, Pallas kernels: 95.1 us -> 91 us  [body(): pl.pallas_call(layer_kernel, out_shape=OUTPUTS, in_specs=[anywhere] * 9,...]
where the time goes in v2:
time: 93.8 us; the launch traced here: 93.7 us
  Pallas kernels  93.1 us (99%)
    pallas_call x1, Pallas kernels, body(): pl.pallas_call(layer_kernel, out_shape=OUTPUTS, in_specs=[anywhere] * 9,...  91 us
    pallas_call x1, Pallas kernels, body(): pl.pallas_call(hand_over, out_shape=OUTPUTS, in_specs=[pl.BlockSpec(memor...  2.05 us

profile of v2, /device:TPU:2, one launch (start us, length us, event | category | flops | bytes accessed | tf_op | source)
XLA Modules:
  0.0 93.7 jit_solution(1094605737038453875)
XLA Ops:
  0.6 91.0 %sage_layer.1 = (bf16[256,256]{1,0:T(8,128)(2,1)}, bf16[256,256]{1,0:T(8,128)(2,1)}, f32[256,256]{1,0:T(8,128)}, f32[256,256]{1,0:T(8,128)}, f32[256]{0:T(256)}) custom-call(bf16[256,256]{1,0:T(8,128)(2,1)} %features.1, bf16[1,256,128,128]{3,2,1,0:T(8,128)(2,1)} %bitcast.1, s32[1,16,16]{2,1,0:T(8,128)} %rest_0_.1, s32[1,16,16]{2,1,0:T(8,128)} %rest_1_.1, ...), custom_call_target="tpu_custom_call" | custom-call | tf_op jit(solution)/shard_map/sage_layer/pallas_call | solution.py:556
  91.6 2.1 %hand_over.1 = (bf16[256,256]{1,0:T(8,128)(2,1)}, bf16[256,256]{1,0:T(8,128)(2,1)}, f32[256,256]{1,0:T(8,128)}, f32[256,256]{1,0:T(8,128)}, f32[256]{0:T(256)}) custom-call(bf16[256,256]{1,0:T(8,128)(2,1)} %get-tuple-element.10.refs_0_, bf16[256,256]{1,0:T(8,128)(2,1)} %get-tuple-element.11.refs_1_, f32[256,256]{1,0:T(8,128)} %get-tuple-element.12.refs_2_, ...), custom_call_target="tpu_custom_call" | custom-call | tf_op jit(solution)/shard_map/hand_over/pallas_call | solution.py:569

commit v3 on v2

--- a/solution.py
+++ b/solution.py
@@ -492,12 +492,15 @@
                 y0_out[way, k] = chip_term(0, j, way).astype(BF)
                 w.push("p%d%d" % (way, k), y0_out.at[way, k], y0_in.at[way, k], device)
 
-    def neighbours(g):
+    def near(g):
         k = groups[g][0][0]
         for way, device in enumerate((y_up, y_down)):
             w.take("k%d%d" % (g, way), core_in.at[g, way])
             y1_out[way, k, 1 - way] = chip_term(g, way, 1 - way).astype(BF)
             w.push("q%d%d%d" % (way, k, 1 - way), y1_out.at[way, k, 1 - way], y1_in.at[way, k, 1 - way], device)
+
+    def late(g):
+        k = groups[g][0][0]
         for way, device in enumerate((y_up, y_down)):
             w.take("p%d%d" % (way, k), y0_in.at[way, k])
             y1_out[way, k, way] = (chip_term(g, way, way) + y0_in[way, k].astype(F32)).astype(BF)
@@ -516,12 +519,14 @@
     opposite()
     for_mate(2)
     for_own(1)
-    neighbours(1)
-    weights_total()
+    near(1)
     for_mate(3)
     for_own(2)
-    neighbours(2)
+    near(2)
+    late(1)
+    weights_total()
     for_own(3)
+    late(2)
     w.take("k30", core_in.at[3, 0])
     w.take("k31", core_in.at[3, 1])
     for half in range(2):

time: 93.8 us -> 94.7 us (level)
  no operation moved by 1% of the time
where the time goes in v3:
time: 94.7 us; the launch traced here: 94.5 us
  Pallas kernels  93.8 us (99%)
    pallas_call x1, Pallas kernels, body(): pl.pallas_call(layer_kernel, out_shape=OUTPUTS, in_specs=[anywhere] * 9,...  91.8 us
    pallas_call x1, Pallas kernels, body(): pl.pallas_call(hand_over, out_shape=OUTPUTS, in_specs=[pl.BlockSpec(memor...  2.05 us

profile of v3, /device:TPU:2, one launch (start us, length us, event | category | flops | bytes accessed | tf_op | source)
XLA Modules:
  0.0 94.5 jit_solution(980156362364361490)
XLA Ops:
  0.6 91.8 %sage_layer.1 = (bf16[256,256]{1,0:T(8,128)(2,1)}, bf16[256,256]{1,0:T(8,128)(2,1)}, f32[256,256]{1,0:T(8,128)}, f32[256,256]{1,0:T(8,128)}, f32[256]{0:T(256)}) custom-call(bf16[256,256]{1,0:T(8,128)(2,1)} %features.1, bf16[1,256,128,128]{3,2,1,0:T(8,128)(2,1)} %bitcast.1, s32[1,16,16]{2,1,0:T(8,128)} %rest_0_.1, s32[1,16,16]{2,1,0:T(8,128)} %rest_1_.1, ...), custom_call_target="tpu_custom_call" | custom-call | tf_op jit(solution)/shard_map/sage_layer/pallas_call | solution.py:561
  92.4 2.1 %hand_over.1 = (bf16[256,256]{1,0:T(8,128)(2,1)}, bf16[256,256]{1,0:T(8,128)(2,1)}, f32[256,256]{1,0:T(8,128)}, f32[256,256]{1,0:T(8,128)}, f32[256]{0:T(256)}) custom-call(bf16[256,256]{1,0:T(8,128)(2,1)} %get-tuple-element.10.refs_0_, bf16[256,256]{1,0:T(8,128)(2,1)} %get-tuple-element.11.refs_1_, f32[256,256]{1,0:T(8,128)} %get-tuple-element.12.refs_2_, ...), custom_call_target="tpu_custom_call" | custom-call | tf_op jit(solution)/shard_map/hand_over/pallas_call | solution.py:574
